TPU v7x, 512 devices: a whole 4x8x8 slice. The times are simulated.
512 devices in a mesh: vol: 32 (over x, z), nar: 16 (over y, core).
Axes of the slice: x: 4, y: 8, z: 8, core: 2. Of those that a mesh axis runs over, the one named last changes fastest.
Arguments:
- series: bfloat16 [32768, 2048], P(('vol', 'nar')), may hold values from -6 to 6
- send_rows: int32 [32, 16, 64], P('vol', 'nar'), may hold values from -1 to 63, as said below
- bin_counts: int32 [16], replicated, may hold values from 1 to 32, 256 in all
- observer_cells: int32 [2, 512], replicated, may hold values from 0 to 127
Outputs:
- spectra_out: float32 [16, 32, 2, 512], P('nar', 'vol')
Inputs may be any that keep to these rules, and one draw needn't show every extreme that they name: `send_rows`: entry (u, n, k) names the row of device (u, n)'s 64 rows of series for slot k mod 2 bound for the patch owner at vol index k // 2 and nar index n, or is -1 for an empty slot; one device never names a row twice. Nar index m owns bin_counts[m] bins in order, from the sum of the counts before m on; some owner holds exactly 32 bins. `observer_cells`: row 0 holds polar indices, row 1 azimuthal indices.
All inputs are finite; a program needn't handle non-finite values.
Results may differ from a plain program's by a relative error of at most 0.0043.
Values may be sent and summed in bfloat16 or wider, within the bound.
A program may use at most 64 MiB of HBM per device.

v0:
```python
import math
import jax
import jax.numpy as jnp
from jax import lax
from jax.sharding import PartitionSpec as P

NF = 256
NQ = 4
WAVE_STEP = 0.05


def dft_table(bin_ids, keep_bin, time_len):
    time_steps = jnp.arange(time_len, dtype=jnp.int32)
    frequency = bin_ids + 1
    phase_turns = time_steps[:, None] * frequency[None, :] % time_len
    angle_grid = phase_turns.astype(jnp.float32) * (2.0 * math.pi / time_len)
    dft_grid = jnp.stack([jnp.cos(angle_grid), -jnp.sin(angle_grid)], axis=-1)
    dft_grid = jnp.where(keep_bin[None, :, None], dft_grid, jnp.float32(0.0))
    return dft_grid.reshape(time_len, 2 * bin_ids.shape[0]).astype(jnp.bfloat16)


def positions(point_list):
    beside_all = (point_list * 1597 % 8191).astype(jnp.float32) * (2.0 * math.pi / 8191.0)
    jitter = (point_list * 613 % 127).astype(jnp.float32) * (0.37 / 127.0)
    axial = (point_list // 128).astype(jnp.float32) * 0.5 + jitter
    return (20.0 * jnp.cos(beside_all), 20.0 * jnp.sin(beside_all), axial)


def directions(obs_cells):
    polar_angle = (obs_cells[0].astype(jnp.float32) + 0.5) * (math.pi / 128.0)
    azimuth = obs_cells[1].astype(jnp.float32) * (2.0 * math.pi / 128.0)
    return (
        jnp.sin(polar_angle) * jnp.cos(azimuth),
        jnp.sin(polar_angle) * jnp.sin(azimuth),
        jnp.cos(polar_angle),
    )


def project(facing, place_xyz):
    dotted = facing[0][:, None] * place_xyz[0][None, :] + facing[1][:, None] * place_xyz[1][None, :]
    return dotted + facing[2][:, None] * place_xyz[2][None, :]


def kernels(bin_ids, dotted):
    wavenumber = (bin_ids.astype(jnp.float32) + 1.0) * WAVE_STEP
    phase_grid = wavenumber[:, None, None] * dotted[None]
    return jnp.concatenate([jnp.cos(phase_grid), jnp.sin(phase_grid)], axis=1).astype(jnp.bfloat16)


def combine(products, bin_ids, facing, norm_scale):
    observers = facing[0].shape[0]
    bin_total = bin_ids.shape[0]
    cos_part = products[:, :observers].reshape(bin_total, observers, NQ, 2)
    sine_part = products[:, observers:].reshape(bin_total, observers, NQ, 2)
    real_part = cos_part[..., 0] + sine_part[..., 1]
    imag_part = cos_part[..., 1] - sine_part[..., 0]
    weights = jnp.stack([jnp.ones_like(facing[0]), facing[0], facing[1], facing[2]], axis=-1)
    real_sum = jnp.sum(real_part * weights[None], axis=-1)
    imag_sum = jnp.sum(imag_part * weights[None], axis=-1)
    amplitude = (bin_ids.astype(jnp.float32) + 1.0) * (norm_scale / NF)
    return jnp.stack([-amplitude[:, None] * imag_sum, amplitude[:, None] * real_sum], axis=1)


def apply_green(bin_ids, spec_block, dotted, facing, norm_scale):
    green_grid = kernels(bin_ids, dotted)
    products = jnp.einsum(
        "bxp,bcp->bxc", green_grid, spec_block, preferred_element_type=jnp.float32
    )
    return combine(products, bin_ids, facing, norm_scale)


def per_device(series, send_rows, bin_counts, observer_cells):
    vol_count = lax.axis_size("vol")
    nar_count = lax.axis_size("nar")
    vol_index = lax.axis_index("vol")
    nar_index = lax.axis_index("nar")
    bin_cap = vol_count * max(1, 2 * NF // (nar_count * vol_count))
    time_len = series.shape[1] // NQ
    slot_total = send_rows.shape[2]
    slot_width = slot_total // vol_count
    listing = send_rows.reshape(-1)
    picked = jnp.take(series, jnp.maximum(listing, 0), axis=0)
    packed = jnp.where((listing >= 0)[:, None], picked, jnp.zeros((), series.dtype))
    arrived = lax.all_to_all(packed, "vol", split_axis=0, concat_axis=0, tiled=True)
    owners = jnp.arange(bin_counts.shape[0], dtype=jnp.int32)
    starts = jnp.sum(jnp.where(owners[None, :] < owners[:, None], bin_counts[None, :], 0), axis=1)
    own_start = starts[nar_index]
    own_count = bin_counts[nar_index]
    dft_scale = 1.0 / math.sqrt(time_len)
    within = jnp.arange(bin_cap, dtype=jnp.int32)
    own_table = dft_table(own_start + within, within < own_count, time_len)
    row_piece = lax.all_gather(arrived, "nar", axis=0, tiled=True)
    rows_here = row_piece.shape[0]
    spectral = jnp.dot(
        row_piece.reshape(rows_here * NQ, time_len), own_table, preferred_element_type=jnp.float32
    )
    spectral = (spectral * dft_scale).astype(jnp.bfloat16).reshape(rows_here, NQ, bin_cap, 2)
    spectra = spectral.transpose(2, 1, 3, 0).reshape(bin_cap, 2 * NQ, rows_here)
    local_points = nar_count * slot_total
    norm_scale = 1.0 / math.sqrt(vol_count * nar_count * slot_total)
    facing = directions(observer_cells)
    share_rows = bin_cap // vol_count
    local_index = jnp.arange(local_points, dtype=jnp.int32)
    nar_source = local_index // slot_total
    remain = local_index % slot_total
    vol_source = remain // slot_width
    within_slot = remain % slot_width
    dotted = project(
        facing,
        positions(
            ((vol_source * nar_count + nar_source) * vol_count + vol_index) * slot_width
            + within_slot
        ),
    )
    row_count = lax.axis_size("vol") * share_rows
    bin_ids = own_start + jnp.arange(row_count, dtype=jnp.int32)
    group_size = 4

    def one_group(bundle):
        return apply_green(bundle[0], bundle[1], dotted, facing, norm_scale)

    grouped = lax.map(
        one_group,
        (
            bin_ids.reshape(row_count // group_size, group_size),
            spectra.reshape(row_count // group_size, group_size, 2 * NQ, local_points),
        ),
    )
    result = lax.psum_scatter(
        grouped.reshape(row_count, 2, grouped.shape[-1]), "vol", scatter_dimension=0, tiled=True
    )
    return result.reshape(1, share_rows, 2, result.shape[-1])


def solution(mesh):
    placed = (P(("vol", "nar"), None), P("vol", "nar", None), P(), P())
    return jax.shard_map(
        per_device,
        mesh=mesh,
        in_specs=placed,
        out_specs=P("nar", "vol", None, None),
        check_vma=False,
    )
```

profile of v0, /device:TPU:2, one launch (start us, length us, event | category | flops | bytes accessed | tf_op | source)
XLA Modules:
  0.0 570.2 jit_solution(7195838264246418794)
XLA Ops:
  9.5 24.5 %all_to_all.9 = bf16[32,2,2048]{2,1,0:T(2,128)(2,1)S(1)} all-to-all(bf16[32,2,2048]{2,1,0:T(2,128)(2,1)S(1)} %broadcast_select_fusion.1), channel_id=1, replica_groups=mesh['vol'=32,'nar'=16] {'vol'}, dimensions={0} | all-to-all | bytes 524288 | tf_op jit(solution)/shard_map/all_to_all | solution.py:84
  39.1 37.2 %all-gather.2.cloned.1.call-done = bf16[1024,2048]{1,0:T(8,128)(2,1)} async-done(((bf16[64,2048]{1,0:T(8,128)(2,1)}), bf16[1024,2048]{1,0:T(8,128)(2,1)}) %all-gather.2.cloned.1.call-update) | async-done | bytes 4194320 | tf_op jit(solution)/shard_map/all_gather | solution.py:92
  76.3 7.6 %reshape.422 = bf16[4096,512]{1,0:T(8,128)(2,1)} reshape(bf16[1024,2048]{1,0:T(8,128)(2,1)} %all-gather.2.cloned.1.call-done) | data formatting | bytes 8388608 | tf_op jit(solution)/shard_map/reshape | solution.py:95
  83.9 3.6 fusion.19
  87.5 37.2 %reshape.423 = bf16[1024,4,32,2]{1,0,3,2:T(8,128)(2,1)} reshape(bf16[4096,64]{0,1:T(8,128)(2,1)S(1)} %fusion.19) | data formatting | bytes 1048576 | tf_op jit(solution)/shard_map/reshape | solution.py:97
  124.7 13.5 %copy.22 = bf16[32,4,2,1024]{3,2,1,0:T(2,128)(2,1)S(1)} copy(bf16[32,4,2,1024]{1,3,2,0:T(8,128)(2,1)} %bitcast.64) | data formatting | bytes 1048576 | tf_op jit(solution)/shard_map/transpose | solution.py:98
  138.4 270.9 %while.12 = (s32[]{:T(128)}, f32[8,4,2,512]{3,2,1,0:T(2,128)S(1)}, s32[8,4]{1,0:T(8,128)S(1)}, bf16[8,4,8,1024]{3,2,1,0:T(8,128)(2,1)S(1)}, f32[512]{0:T(512)S(1...) while((s32[]{:T(128)}, f32[8,4,2,512]{3,2,1,0:T(2,128)S(1)}, ...), condition=%wide.region_4.5_spmd.clone.clone, body=%wide.region_1.4_spmd.clone.clone.sunk | while | flops 92858400 | bytes 22143284 | solution.py:122
  138.9 30.2 %fusion.74 = (bf16[4,512,1024]{2,1,0:T(8,128)(2,1)S(1)}, bf16[4,512,1024]{2,1,0:T(8,128)(2,1)S(1)}) fusion(f32[512,1024]{1,0:T(8,128)S(1)} %multiply_add_fusion.2, f32[4]{0:T(128)S(1)} %multiply_bitcast_fusion.4), kind=kLoop, calls=%fused_computation.4.clone.1 | loop fusion | flops 6291456 | bytes 10485776 | tf_op jit(solution)/shard_map/convert
  169.1 2.6 fusion.75
  172.8 30.2 %fusion.74 = (bf16[4,512,1024]{2,1,0:T(8,128)(2,1)S(1)}, bf16[4,512,1024]{2,1,0:T(8,128)(2,1)S(1)}) fusion(f32[512,1024]{1,0:T(8,128)S(1)} %multiply_add_fusion.2, f32[4]{0:T(128)S(1)} %multiply_bitcast_fusion.4), kind=kLoop, calls=%fused_computation.4.clone.1 | loop fusion | flops 6291456 | bytes 10485776 | tf_op jit(solution)/shard_map/convert
  203.0 2.6 fusion.75
  206.6 30.2 %fusion.74 = (bf16[4,512,1024]{2,1,0:T(8,128)(2,1)S(1)}, bf16[4,512,1024]{2,1,0:T(8,128)(2,1)S(1)}) fusion(f32[512,1024]{1,0:T(8,128)S(1)} %multiply_add_fusion.2, f32[4]{0:T(128)S(1)} %multiply_bitcast_fusion.4), kind=kLoop, calls=%fused_computation.4.clone.1 | loop fusion | flops 6291456 | bytes 10485776 | tf_op jit(solution)/shard_map/convert
  236.9 2.6 fusion.75
  240.5 30.2 %fusion.74 = (bf16[4,512,1024]{2,1,0:T(8,128)(2,1)S(1)}, bf16[4,512,1024]{2,1,0:T(8,128)(2,1)S(1)}) fusion(f32[512,1024]{1,0:T(8,128)S(1)} %multiply_add_fusion.2, f32[4]{0:T(128)S(1)} %multiply_bitcast_fusion.4), kind=kLoop, calls=%fused_computation.4.clone.1 | loop fusion | flops 6291456 | bytes 10485776 | tf_op jit(solution)/shard_map/convert
  270.7 2.6 fusion.75
  274.3 30.2 %fusion.74 = (bf16[4,512,1024]{2,1,0:T(8,128)(2,1)S(1)}, bf16[4,512,1024]{2,1,0:T(8,128)(2,1)S(1)}) fusion(f32[512,1024]{1,0:T(8,128)S(1)} %multiply_add_fusion.2, f32[4]{0:T(128)S(1)} %multiply_bitcast_fusion.4), kind=kLoop, calls=%fused_computation.4.clone.1 | loop fusion | flops 6291456 | bytes 10485776 | tf_op jit(solution)/shard_map/convert
  304.6 2.6 fusion.75
  308.2 30.2 %fusion.74 = (bf16[4,512,1024]{2,1,0:T(8,128)(2,1)S(1)}, bf16[4,512,1024]{2,1,0:T(8,128)(2,1)S(1)}) fusion(f32[512,1024]{1,0:T(8,128)S(1)} %multiply_add_fusion.2, f32[4]{0:T(128)S(1)} %multiply_bitcast_fusion.4), kind=kLoop, calls=%fused_computation.4.clone.1 | loop fusion | flops 6291456 | bytes 10485776 | tf_op jit(solution)/shard_map/convert
  338.4 2.6 fusion.75
  342.1 30.2 %fusion.74 = (bf16[4,512,1024]{2,1,0:T(8,128)(2,1)S(1)}, bf16[4,512,1024]{2,1,0:T(8,128)(2,1)S(1)}) fusion(f32[512,1024]{1,0:T(8,128)S(1)} %multiply_add_fusion.2, f32[4]{0:T(128)S(1)} %multiply_bitcast_fusion.4), kind=kLoop, calls=%fused_computation.4.clone.1 | loop fusion | flops 6291456 | bytes 10485776 | tf_op jit(solution)/shard_map/convert
  372.3 2.6 fusion.75
  375.9 30.2 %fusion.74 = (bf16[4,512,1024]{2,1,0:T(8,128)(2,1)S(1)}, bf16[4,512,1024]{2,1,0:T(8,128)(2,1)S(1)}) fusion(f32[512,1024]{1,0:T(8,128)S(1)} %multiply_add_fusion.2, f32[4]{0:T(128)S(1)} %multiply_bitcast_fusion.4), kind=kLoop, calls=%fused_computation.4.clone.1 | loop fusion | flops 6291456 | bytes 10485776 | tf_op jit(solution)/shard_map/convert
  406.2 2.6 fusion.75
  411.3 150.1 %all-reduce.3.cloned.1.call-done = f32[32,2,512]{2,1,0:T(2,128)} async-done(((f32[32,2,512]{2,1,0:T(2,128)}), f32[32,2,512]{2,1,0:T(2,128)}) %all-reduce.3.cloned.1.call-update) | async-done | bytes 131088
  (134 shorter events, 19.3 us)
Async XLA Ops:
  6.5 1.6 copy-start
  6.5 28.4 %copy-start.3 = (s32[16]{0:T(128)S(1)}, s32[16]{0:T(128)}, u32[]{:S(2)}) copy-start(s32[16]{0:T(128)} %param.8) | copy-start | bytes 196
  6.5 32.4 %copy-start.2 = (s32[2,512]{1,0:T(2,128)S(1)}, s32[2,512]{1,0:T(2,128)}, u32[]{:S(2)}) copy-start(s32[2,512]{1,0:T(2,128)} %param.9) | copy-start | bytes 12292
  6.5 69.8 %all-gather.2.cloned.1.call-start = ((), (), s32[]{:S(2)}) async-start(), calls=%async_computation.1 | async-start | bytes 4456448 | tf_op jit(solution)/shard_map/all_gather | solution.py:92
  34.9 526.5 %all-reduce.3.cloned.1.call-start = ((), (), s32[]{:S(2)}) async-start(), calls=%async_computation.2 | async-start | bytes 262144
  409.3 0.6 copy-start.1
Sparse Core Ops, SparseCore 0:
  35.0 41.2 all-gather.1
  410.1 151.2 all-reduce.2
where the time goes:
time: 571 us; the launch traced here: 570 us
  other arithmetic  253 us (44%)
  waiting for transfers between devices  187 us (33%)
  local copies, waits for them, and re-layouts  66.6 us (12%)
  matrix products  24.7 us (4%)
  blocking collectives  24.5 us (4%)
  between operations  13.6 us (2%)
    another operation x8, other arithmetic  242 us
    unnamed x3, waiting for transfers between devices  150 us
    all_gather x1, waiting for transfers between devices, per_device(): row_piece = lax.all_gather(arrived, 'nar', axis=0, tiled=True)  37.2 us
    reshape x1, local copies, waits for them, and re-layouts, per_device(): (spectral * dft_scale).astype(jnp.bfloat16)  37.2 us
    all_to_all x1, blocking collectives, per_device(): lax.all_to_all(packed, 'vol', split_axis=0, concat_axis=0, tiled=True)  24.5 us
    dot_general x8, matrix products, apply_green(): jnp.einsum('bxp,bcp->bxc', green_grid, spec_block, preferred_element_type...  21.1 us
    transpose x1, local copies, waits for them, and re-layouts, per_device(): spectra = spectral.transpose(2, 1, 3, 0).reshape(bin_cap, 2 * NQ, rows_here)  13.5 us
  transfers between devices with their start and end apart: 2, of which 2 were waited for; matrix products, arithmetic and copies ran while one was open for 1% of the time, Pallas kernels for 0%

commit v1 on v0

--- a/solution.py
+++ b/solution.py
@@ -89,7 +89,9 @@
     dft_scale = 1.0 / math.sqrt(time_len)
     within = jnp.arange(bin_cap, dtype=jnp.int32)
     own_table = dft_table(own_start + within, within < own_count, time_len)
-    row_piece = lax.all_gather(arrived, "nar", axis=0, tiled=True)
+    row_piece = jnp.concatenate(
+        lax.all_to_all(jnp.stack([arrived] * lax.axis_size("nar")), "nar", 0, 0), axis=0
+    )
     rows_here = row_piece.shape[0]
     spectral = jnp.dot(
         row_piece.reshape(rows_here * NQ, time_len), own_table, preferred_element_type=jnp.float32

time: 571 us -> 628 us (1.100)
  waiting for transfers between devices: 187 us -> 236 us
  starting transfers between devices: 0.04 us -> 7.43 us
    all_to_all x0 -> x1, waiting for transfers between devices: none -> 90.3 us  [per_device(): lax.all_to_all(jnp.stack([arrived] * lax.axis_size('nar')), 'nar', 0, 0)]
    all_gather x1 -> x0, waiting for transfers between devices: 37.2 us -> none  [per_device(): row_piece = lax.all_gather(arrived, 'nar', axis=0, tiled=True)]
    another operation x0 -> x3, local copies, waits for them, and re-layouts: none -> 10.2 us  [the longest x1 7.57 us: per_device(): row_piece.reshape(rows_here * NQ, time_len)]
    reshape x1 -> x0, local copies, waits for them, and re-layouts: 7.57 us -> none  [per_device(): row_piece.reshape(rows_here * NQ, time_len)]
    all_to_all x0 -> x1, starting transfers between devices: none -> 7.39 us  [per_device(): lax.all_to_all(jnp.stack([arrived] * lax.axis_size('nar')), 'nar', 0, 0)]
    unnamed x3 -> x2, waiting for transfers between devices: 150 us -> 145 us
where the time goes in v1:
time: 628 us; the launch traced here: 627 us
  other arithmetic  253 us (40%)
  waiting for transfers between devices  236 us (38%)
  local copies, waits for them, and re-layouts  68.3 us (11%)
  matrix products  24.7 us (4%)
  blocking collectives  24.5 us (4%)
  between operations  13.6 us (2%)
  starting transfers between devices  7.43 us (1%)
    another operation x8, other arithmetic  242 us
    unnamed x2, waiting for transfers between devices  145 us
    all_to_all x1, waiting for transfers between devices, per_device(): lax.all_to_all(jnp.stack([arrived] * lax.axis_size('nar')), 'nar', 0, 0)  90.3 us
    reshape x1, local copies, waits for them, and re-layouts, per_device(): (spectral * dft_scale).astype(jnp.bfloat16)  37.2 us
    all_to_all x1, blocking collectives, per_device(): lax.all_to_all(packed, 'vol', split_axis=0, concat_axis=0, tiled=True)  24.5 us
    dot_general x8, matrix products, apply_green(): jnp.einsum('bxp,bcp->bxc', green_grid, spec_block, preferred_element_type...  21.1 us
    transpose x1, local copies, waits for them, and re-layouts, per_device(): spectra = spectral.transpose(2, 1, 3, 0).reshape(bin_cap, 2 * NQ, rows_here)  13.5 us
  transfers between devices with their start and end apart: 2, of which 2 were waited for; matrix products, arithmetic and copies ran while one was open for 1% of the time, Pallas kernels for 0%

profile of v1, /device:TPU:2, one launch (start us, length us, event | category | flops | bytes accessed | tf_op | source)
XLA Modules:
  0.0 627.4 jit_solution(2845284111568236255)
XLA Ops:
  9.5 24.5 %all_to_all.11 = bf16[32,2,2048]{2,1,0:T(2,128)(2,1)S(1)} all-to-all(bf16[32,2,2048]{2,1,0:T(2,128)(2,1)S(1)} %broadcast_select_fusion.1), channel_id=1, replica_groups=mesh['vol'=32,'nar'=16] {'vol'}, dimensions={0} | all-to-all | bytes 524288 | tf_op jit(solution)/shard_map/all_to_all | solution.py:84
  36.7 7.4 %all-to-all-start.1 = ((bf16[16,64,2048]{2,1,0:T(8,128)(2,1)}), bf16[16,64,2048]{2,1,0:T(8,128)(2,1)}, u32[]{:S(2)}, u32[]{:S(2)}) async-start(bf16[16,64,2048]{2,1,0:T(8,128)(2,1)} %stack.17), calls=%async_computation.1 | async-start | bytes 8388608 | tf_op jit(solution)/shard_map/all_to_all | solution.py:93
  48.1 90.3 %all-to-all-done.1 = bf16[16,64,2048]{2,1,0:T(8,128)(2,1)} async-done(((bf16[16,64,2048]{2,1,0:T(8,128)(2,1)}), bf16[16,64,2048]{2,1,0:T(8,128)(2,1)}, u32[]{:S(2)}, u32[]{:S(2)}) %all-to-all-start.1) | async-done | bytes 4194336 | tf_op jit(solution)/shard_map/all_to_all | solution.py:93
  138.4 7.6 %reshape_reshape.6 = bf16[4096,512]{1,0:T(8,128)(2,1)} reshape(bf16[16,64,2048]{2,1,0:T(8,128)(2,1)} %all-to-all-done.1) | data formatting | bytes 8388608 | tf_op jit(solution)/shard_map/reshape;reshape | solution.py:97
  146.0 3.6 fusion.19
  149.5 37.2 %reshape.422 = bf16[1024,4,32,2]{1,0,3,2:T(8,128)(2,1)} reshape(bf16[4096,64]{0,1:T(8,128)(2,1)S(1)} %fusion.19) | data formatting | bytes 1048576 | tf_op jit(solution)/shard_map/reshape | solution.py:99
  186.7 13.5 %copy.22 = bf16[32,4,2,1024]{3,2,1,0:T(2,128)(2,1)S(1)} copy(bf16[32,4,2,1024]{1,3,2,0:T(8,128)(2,1)} %bitcast.64) | data formatting | bytes 1048576 | tf_op jit(solution)/shard_map/transpose | solution.py:100
  200.5 270.9 %while.12 = (s32[]{:T(128)}, f32[8,4,2,512]{3,2,1,0:T(2,128)S(1)}, s32[8,4]{1,0:T(8,128)S(1)}, bf16[8,4,8,1024]{3,2,1,0:T(8,128)(2,1)S(1)}, f32[512]{0:T(512)S(1...) while((s32[]{:T(128)}, f32[8,4,2,512]{3,2,1,0:T(2,128)S(1)}, ...), condition=%wide.region_4.5_spmd.clone.clone, body=%wide.region_1.4_spmd.clone.clone.sunk | while | flops 92858400 | bytes 22143284 | solution.py:124
  200.9 30.2 %fusion.74 = (bf16[4,512,1024]{2,1,0:T(8,128)(2,1)S(1)}, bf16[4,512,1024]{2,1,0:T(8,128)(2,1)S(1)}) fusion(f32[512,1024]{1,0:T(8,128)S(1)} %multiply_add_fusion.2, f32[4]{0:T(128)S(1)} %multiply_bitcast_fusion.4), kind=kLoop, calls=%fused_computation.4.clone.1 | loop fusion | flops 6291456 | bytes 10485776 | tf_op jit(solution)/shard_map/convert
  231.2 2.6 fusion.75
  234.8 30.2 %fusion.74 = (bf16[4,512,1024]{2,1,0:T(8,128)(2,1)S(1)}, bf16[4,512,1024]{2,1,0:T(8,128)(2,1)S(1)}) fusion(f32[512,1024]{1,0:T(8,128)S(1)} %multiply_add_fusion.2, f32[4]{0:T(128)S(1)} %multiply_bitcast_fusion.4), kind=kLoop, calls=%fused_computation.4.clone.1 | loop fusion | flops 6291456 | bytes 10485776 | tf_op jit(solution)/shard_map/convert
  265.0 2.6 fusion.75
  268.7 30.2 %fusion.74 = (bf16[4,512,1024]{2,1,0:T(8,128)(2,1)S(1)}, bf16[4,512,1024]{2,1,0:T(8,128)(2,1)S(1)}) fusion(f32[512,1024]{1,0:T(8,128)S(1)} %multiply_add_fusion.2, f32[4]{0:T(128)S(1)} %multiply_bitcast_fusion.4), kind=kLoop, calls=%fused_computation.4.clone.1 | loop fusion | flops 6291456 | bytes 10485776 | tf_op jit(solution)/shard_map/convert
  298.9 2.6 fusion.75
  302.5 30.2 %fusion.74 = (bf16[4,512,1024]{2,1,0:T(8,128)(2,1)S(1)}, bf16[4,512,1024]{2,1,0:T(8,128)(2,1)S(1)}) fusion(f32[512,1024]{1,0:T(8,128)S(1)} %multiply_add_fusion.2, f32[4]{0:T(128)S(1)} %multiply_bitcast_fusion.4), kind=kLoop, calls=%fused_computation.4.clone.1 | loop fusion | flops 6291456 | bytes 10485776 | tf_op jit(solution)/shard_map/convert
  332.8 2.6 fusion.75
  336.4 30.2 %fusion.74 = (bf16[4,512,1024]{2,1,0:T(8,128)(2,1)S(1)}, bf16[4,512,1024]{2,1,0:T(8,128)(2,1)S(1)}) fusion(f32[512,1024]{1,0:T(8,128)S(1)} %multiply_add_fusion.2, f32[4]{0:T(128)S(1)} %multiply_bitcast_fusion.4), kind=kLoop, calls=%fused_computation.4.clone.1 | loop fusion | flops 6291456 | bytes 10485776 | tf_op jit(solution)/shard_map/convert
  370.2 30.2 %fusion.74 = (bf16[4,512,1024]{2,1,0:T(8,128)(2,1)S(1)}, bf16[4,512,1024]{2,1,0:T(8,128)(2,1)S(1)}) fusion(f32[512,1024]{1,0:T(8,128)S(1)} %multiply_add_fusion.2, f32[4]{0:T(128)S(1)} %multiply_bitcast_fusion.4), kind=kLoop, calls=%fused_computation.4.clone.1 | loop fusion | flops 6291456 | bytes 10485776 | tf_op jit(solution)/shard_map/convert
  400.5 2.6 fusion.75
  404.1 30.2 %fusion.74 = (bf16[4,512,1024]{2,1,0:T(8,128)(2,1)S(1)}, bf16[4,512,1024]{2,1,0:T(8,128)(2,1)S(1)}) fusion(f32[512,1024]{1,0:T(8,128)S(1)} %multiply_add_fusion.2, f32[4]{0:T(128)S(1)} %multiply_bitcast_fusion.4), kind=kLoop, calls=%fused_computation.4.clone.1 | loop fusion | flops 6291456 | bytes 10485776 | tf_op jit(solution)/shard_map/convert
  434.3 2.6 fusion.75
  438.0 30.2 %fusion.74 = (bf16[4,512,1024]{2,1,0:T(8,128)(2,1)S(1)}, bf16[4,512,1024]{2,1,0:T(8,128)(2,1)S(1)}) fusion(f32[512,1024]{1,0:T(8,128)S(1)} %multiply_add_fusion.2, f32[4]{0:T(128)S(1)} %multiply_bitcast_fusion.4), kind=kLoop, calls=%fused_computation.4.clone.1 | loop fusion | flops 6291456 | bytes 10485776 | tf_op jit(solution)/shard_map/convert
  468.2 2.6 fusion.75
  473.4 145.2 %all-reduce.3.cloned.1.call-done = f32[32,2,512]{2,1,0:T(2,128)} async-done(((f32[32,2,512]{2,1,0:T(2,128)}), f32[32,2,512]{2,1,0:T(2,128)}) %all-reduce.3.cloned.1.call-update) | async-done | bytes 131088
  (134 shorter events, 23.5 us)
Async XLA Ops:
  6.5 1.6 copy-start
  36.7 7.5 %copy-start.3 = (s32[16]{0:T(128)S(1)}, s32[16]{0:T(128)}, u32[]{:S(2)}) copy-start(s32[16]{0:T(128)} %param.8) | copy-start | bytes 196
  36.7 11.2 %copy-start.2 = (s32[2,512]{1,0:T(2,128)S(1)}, s32[2,512]{1,0:T(2,128)}, u32[]{:S(2)}) copy-start(s32[2,512]{1,0:T(2,128)} %param.9) | copy-start | bytes 12292
  36.7 101.7 %all-to-all-start.1 = ((bf16[16,64,2048]{2,1,0:T(8,128)(2,1)}), bf16[16,64,2048]{2,1,0:T(8,128)(2,1)}, u32[]{:S(2)}, u32[]{:S(2)}) async-start(bf16[16,64,2048]{2,1,0:T(8,128)(2,1)} %stack.17), calls=%async_computation.1 | async-start | bytes 8388608 | tf_op jit(solution)/shard_map/all_to_all | solution.py:93
  44.1 574.5 %all-reduce.3.cloned.1.call-start = ((), (), s32[]{:S(2)}) async-start(), calls=%async_computation.2 | async-start | bytes 262144
  471.4 0.6 copy-start.1
Sparse Core Ops, SparseCore 0:
  472.1 146.3 all-reduce.2
